TPU v7x, 256 devices: a whole 4x4x8 slice. The times are simulated.
256 devices in a mesh: lat: 8 (over x, y_lo), lon: 32 (over z, y_hi, core).
Axes of the slice: x: 4, y: 4 (y_hi: 2, y_lo: 2; y = y_hi * 2 + y_lo), z: 8, core: 2. Of those that a mesh axis runs over, the one named last changes fastest.
Arguments:
- inputs: bfloat16 [128, 4096, 64], P('lat', 'lon'), may hold values from -6 to 6
- pre_first: bfloat16 [128, 4096, 128], P('lat', 'lon'), may hold values from -6 to 6
- grad_out: bfloat16 [64, 2048, 128], P('lat', 'lon'), may hold values from -6 to 6
- w_first: bfloat16 [3, 3, 64, 128], replicated, may hold values from -0.25 to 0.25
- w_second: bfloat16 [3, 3, 128, 128], replicated, may hold values from -0.1875 to 0.1875
Outputs:
- grad_inputs: bfloat16 [128, 4096, 64], P('lat', 'lon')
- grad_w_first: float32 [3, 3, 64, 128], replicated
- grad_w_second: float32 [3, 3, 128, 128], replicated
All inputs are finite; a program needn't handle non-finite values.
Results may differ from a plain program's by a relative error of at most 0.0049.
Values may be sent and summed in bfloat16 or wider, within the bound.
A program may use at most 64 MiB of HBM per device.

v0:
```python
import jax
import jax.numpy as jnp
from jax import lax
from jax.sharding import PartitionSpec as P

inv_root = 0.7071067811865476
density = 0.3989422804014327


def passed_along(shard, axis, by):
    peers = lax.axis_size(axis)
    return lax.ppermute(shard, axis, [(i, (i + by) % peers) for i in range(peers)])


def extended(block, sides, width):
    for axis, dim in sides:
        count = lax.axis_size(axis)
        forward = [(i, i + 1) for i in range(count - 1)]
        forward.append((count - 1, 0))
        backward = [(target, source) for source, target in forward]
        low = lax.ppermute(
            lax.slice_in_dim(block, block.shape[dim] - width, None, axis=dim), axis, forward
        )
        high = lax.ppermute(lax.slice_in_dim(block, 0, width, axis=dim), axis, backward)
        block = jnp.concatenate([low, block, high], axis=dim)
    return block


def across_values(row):
    return passed_along(row, "lon", lax.axis_size("lon") // 2)


def across_grads(row):
    return passed_along(row, "lon", lax.axis_size("lon") // 2)


def pad_values(fields):
    band = lax.axis_index("lat")
    padded = extended(fields, (("lat", 0), ("lon", 1)), 1)
    opposite = across_values(padded[1])
    top = jnp.where(band == 0, opposite, padded[0])
    bottom = jnp.where(band == lax.axis_size("lat") - 1, jnp.zeros_like(padded[-1]), padded[-1])
    return jnp.concatenate([top[None], padded[1:-1], bottom[None]], 0)


def fold_grads(grid):
    band = lax.axis_index("lat")
    first = band == 0
    final = band == lax.axis_size("lat") - 1
    opposite = across_grads(grid[0])
    row_one = grid[1] + jnp.where(first, opposite, jnp.zeros_like(opposite))
    top = jnp.where(first, jnp.zeros_like(grid[0]), grid[0])
    bottom = jnp.where(final, jnp.zeros_like(grid[-1]), grid[-1])
    grid = jnp.concatenate([top[None], row_one[None], grid[2:-1], bottom[None]], 0)
    wide = extended(grid, (("lat", 0), ("lon", 1)), 1)
    inner = wide[2:-2]
    inner = inner.at[0].add(wide[0]).at[-1].add(wide[-1])
    core = inner[:, 2:-2]
    core = core.at[:, 0].add(inner[:, 0]).at[:, -1].add(inner[:, -1])
    return core


def taps_product(padded, grads):
    rows, cols = (grads.shape[0], grads.shape[1])
    flat = grads.reshape(rows * cols, grads.shape[2])
    result = []
    for a in range(3):
        line = []
        for b in range(3):
            piece = padded[a : a + rows, b : b + cols].reshape(rows * cols, padded.shape[2])
            line.append(
                lax.dot_general(
                    piece, flat, (((0,), (0,)), ((), ())), preferred_element_type=jnp.float32
                )
            )
        result.append(jnp.stack(line, 0))
    return jnp.stack(result, 0)


def spread(grads, weight):
    rows, cols, cout = grads.shape
    cin = weight.shape[2]
    every = jnp.transpose(weight, (3, 0, 1, 2)).reshape(cout, 9 * cin)
    terms = jnp.dot(grads.reshape(rows * cols, cout), every, preferred_element_type=jnp.float32)
    terms = terms.reshape(rows, cols, 3, 3, cin)
    grid = jnp.zeros((rows + 2, cols + 2, cin), jnp.float32)
    for a in range(3):
        for b in range(3):
            grid = grid.at[a : a + rows, b : b + cols].add(terms[:, :, a, b])
    return grid


def body(inputs, pre_first, grad_out, w_first, w_second):
    first_ch = inputs.shape[2]
    value = pre_first.astype(jnp.float32)
    cdf = 0.5 * (1.0 + lax.erf(value * inv_root))
    activated = (value * cdf).astype(jnp.bfloat16)
    slope = cdf + value * jnp.exp(-0.5 * value * value) * density
    padded = pad_values(jnp.concatenate([inputs, activated], 2))
    padded_in = padded[:, :, :first_ch]
    padded_act = padded[:, :, first_ch:]
    grad_pool = jnp.repeat(jnp.repeat(grad_out, 2, 0), 2, 1) * jnp.asarray(0.25, grad_out.dtype)
    local_second = taps_product(padded_act, grad_pool)
    grad_act = fold_grads(spread(grad_pool, w_second))
    grad_pre = (grad_act * slope).astype(jnp.bfloat16)
    local_first = taps_product(padded_in, grad_pre)
    grad_inputs = fold_grads(spread(grad_pre, w_first)).astype(jnp.bfloat16)
    grad_w_first, grad_w_second = lax.psum((local_first, local_second), ("lat", "lon"))
    return (grad_inputs, grad_w_first, grad_w_second)


def solution(mesh):
    in_specs = (P("lat", "lon", None), P("lat", "lon", None), P("lat", "lon", None), P(), P())
    out_specs = (P("lat", "lon", None), P(), P())
    return jax.shard_map(body, mesh=mesh, in_specs=in_specs, out_specs=out_specs, check_vma=False)
```

profile of v0, /device:TPU:1, one launch (start us, length us, event | category | flops | bytes accessed | tf_op | source)
XLA Modules:
  0.0 447.3 jit_solution(18419216473036246453)
XLA Ops:
  7.2 1.0 broadcast_multiply_fusion
  8.7 1.4 fusion.71
  10.9 1.1 fusion.104
  12.2 1.6 fusion.17
  14.6 3.4 scatter-add.89
  18.0 3.4 add_select_fusion
  21.3 3.5 scatter-add.90
  24.8 1.4 fusion.16
  26.2 1.3 fusion.14
  27.6 2.1 scatter-add.94
  29.7 1.3 fusion.13
  31.1 2.1 scatter-add.95
  33.2 1.4 fusion.12
  34.6 1.4 fusion.10
  36.0 2.1 scatter-add.99
  38.1 1.4 fusion.9
  39.5 2.1 scatter-add.100
  41.6 2.2 collective-permute-start
  43.8 3.9 collective-permute-done
  47.7 7.1 %collective-permute-start.1 = (f32[130,128]{1,0:T(8,128)S(1)}, f32[130,128]{1,0:T(8,128)S(1)}, u32[]{:S(2)}, u32[]{:S(2)}) collective-permute-start(f32[130,128]{1,0:T(8,128)S(1)} %get-tuple-element.325), channel_id=1, source_target_pairs={{0,16},{1,17},{2,18},{3,19},{4,20},{5,21},{6,22},{7,23},{8,24},{9,... | collective-permute-start | bytes 199688 | tf_op jit(solution)/shard_map/ppermute | solution.py:12
  54.8 1.4 collective-permute-start.2
  56.7 1.5 collective-permute-done.2
  58.3 5.8 %collective-permute-start.3 = (f32[20,1,128]{2,1,0:T(1,128)S(1)}, f32[20,1,128]{2,1,0:T(1,128)S(1)}, u32[]{:S(2)}, u32[]{:S(2)}) collective-permute-start(f32[20,1,128]{2,1,0:T(1,128)S(1)} %get-tuple-element.321), channel_id=1, source_target_pairs={{0,1},{1,2},{2,3},{3,4},{4,5},{5,6},{6,7},{7,8},{8,9},{9,10},{10,1... | collective-permute-start | bytes 30728 | tf_op jit(solution)/shard_map/ppermute | solution.py:21
  65.0 3.8 collective-permute-done.4
  71.1 1.6 fusion.8
  73.5 3.0 fusion.69
  76.5 1.1 slice_bitcast_fusion.17
  77.6 3.3 fusion.68
  81.3 3.6 collective-permute-start.11
  84.8 6.0 %scatter-add.110 = f32[18,130,64]{1,2,0:T(8,128)S(1)} dynamic-update-slice(f32[18,130,64]{1,2,0:T(8,128)S(1)} %scatter-add.109, f32[16,128,64]{1,2,0:T(8,128)} %fusion.68, s32[]{:T(128)} %bitcast.10, s32[]{:T(128)} %bitcast.11, s32[]{:T(128)} %constant.655.clone.1) | dynamic-update-slice | bytes 1048580 | tf_op jit(solution)/shard_map/scatter-add | solution.py:89
  90.8 4.0 add_select_fusion.1
  94.8 6.0 %scatter-add.111 = f32[18,130,64]{1,2,0:T(8,128)S(1)} dynamic-update-slice(f32[18,130,64]{1,2,0:T(8,128)S(1)} %scatter-add.110, f32[16,128,64]{1,2,0:T(8,128)} %add_select_fusion.1, s32[]{:T(128)} %bitcast.13, s32[]{:T(128)} %bitcast.14, s32[]{:T(128)} %constant.655.clone.1) | dynamic-update-slice | bytes 1048580 | tf_op jit(solution)/shard_map/scatter-add | solution.py:89
  100.9 1.2 fusion.67
  102.1 2.0 fusion.65
  104.1 4.7 %scatter-add.115 = f32[18,130,64]{1,2,0:T(8,128)S(1)} dynamic-update-slice(f32[18,130,64]{1,2,0:T(8,128)S(1)} %fusion.67, f32[16,128,64]{1,2,0:T(8,128)} %fusion.65, s32[]{:T(128)} %constant.660.clone.1, s32[]{:T(128)} %constant.660.clone.1, s32[]{:T(128)} %constant.655.clone.1) | dynamic-update-slice | bytes 1048580 | tf_op jit(solution)/shard_map/scatter-add | solution.py:89
  108.8 2.0 fusion.64
  110.8 4.7 %scatter-add.116 = f32[18,130,64]{1,2,0:T(8,128)S(1)} dynamic-update-slice(f32[18,130,64]{1,2,0:T(8,128)S(1)} %scatter-add.115, f32[16,128,64]{1,2,0:T(8,128)} %fusion.64, s32[]{:T(128)} %constant.660.clone.1, s32[]{:T(128)} %constant.656.clone.1, s32[]{:T(128)} %constant.655.clone.1) | dynamic-update-slice | bytes 1048580 | tf_op jit(solution)/shard_map/scatter-add | solution.py:89
  115.5 1.2 fusion.63
  116.7 2.0 fusion.61
  118.7 4.7 %scatter-add.120 = f32[18,130,64]{1,2,0:T(8,128)S(1)} dynamic-update-slice(f32[18,130,64]{1,2,0:T(8,128)S(1)} %fusion.63, f32[16,128,64]{1,2,0:T(8,128)} %fusion.61, s32[]{:T(128)} %constant.656.clone.1, s32[]{:T(128)} %constant.660.clone.1, s32[]{:T(128)} %constant.655.clone.1) | dynamic-update-slice | bytes 1048580 | tf_op jit(solution)/shard_map/scatter-add | solution.py:89
  123.4 2.0 fusion.60
  125.4 4.7 %scatter-add.121 = f32[18,130,64]{1,2,0:T(8,128)S(1)} dynamic-update-slice(f32[18,130,64]{1,2,0:T(8,128)S(1)} %scatter-add.120, f32[16,128,64]{1,2,0:T(8,128)} %fusion.60, s32[]{:T(128)} %constant.656.clone.1, s32[]{:T(128)} %constant.656.clone.1, s32[]{:T(128)} %constant.655.clone.1) | dynamic-update-slice | bytes 1048580 | tf_op jit(solution)/shard_map/scatter-add | solution.py:89
  130.2 1.4 convolution_bitcast_fusion.4
  131.6 4.6 %collective-permute-done.5 = f32[1,130,64]{1,2,0:T(8,128)S(1)} collective-permute-done((f32[1,130,64]{1,2,0:T(8,128)S(1)}, f32[1,130,64]{1,2,0:T(8,128)S(1)}, u32[]{:S(2)}, u32[]{:S(2)}) %collective-permute-start.5) | collective-permute-done | bytes 33312 | tf_op jit(solution)/shard_map/ppermute | solution.py:21
  136.3 1.1 collective-permute-start.12
  137.4 4.8 %collective-permute-start.6 = (f32[130,64]{0,1:T(8,128)S(1)}, f32[130,64]{0,1:T(8,128)S(1)}, u32[]{:S(2)}, u32[]{:S(2)}) collective-permute-start(f32[130,64]{0,1:T(8,128)S(1)} %get-tuple-element.330), channel_id=1, source_target_pairs={{0,16},{1,17},{2,18},{3,19},{4,20},{5,21},{6,22},{7,23},{8,24},{9,... | collective-permute-start | bytes 99848 | tf_op jit(solution)/shard_map/ppermute | solution.py:12
  143.2 0.9 copy-done.3
  145.0 1.2 convolution_bitcast_fusion.2
  146.2 1.3 convolution_bitcast_fusion.1
  150.1 0.9 convolution_bitcast_fusion.10
  151.0 5.4 %collective-permute-start.14 = (bf16[130,192]{1,0:T(8,128)(2,1)}, bf16[130,192]{1,0:T(8,128)(2,1)}, u32[]{:S(2)}, u32[]{:S(2)}) collective-permute-start(bf16[130,192]{1,0:T(8,128)(2,1)} %get-tuple-element.326), channel_id=1, source_target_pairs={{0,16},{1,17},{2,18},{3,19},{4,20},{5,21},{6,22},{7,23},{8,24},{9,... | collective-permute-start | bytes 149768 | tf_op jit(solution)/shard_map/ppermute | solution.py:12
  157.7 0.9 convolution_bitcast_fusion.14
  158.7 1.0 convolution_bitcast_fusion.13
  160.5 1.3 fusion.103
  162.1 2.0 copy.59
  165.8 1.8 copy.60
  167.6 1.7 collective-permute-done.9
  169.3 1.8 copy.61
  171.2 1.9 pad_maximum_fusion.1
  173.1 1.0 copy-done.13
  183.4 1.9 scatter-add.129
  186.1 250.8 %all-reduce.5.cloned.1.call-done = (f32[3,3,64,128]{3,2,1,0:T(8,128)}, f32[3,3,128,128]{3,2,1,0:T(8,128)}) async-done(((f32[3,3,64,128]{3,2,1,0:T(8,128)}, f32[3,3,128,128]{3,2,1,0:T(8,128)}), (f32[3,3,64,128]{3,2,1,0:T(8,128)}, f32[3,3,128,128]{3,2,1,0:T(8,128)})) %all-reduce.5.cloned.1.call-update) | async-done | bytes 884752 | tf_op jit(solution)/shard_map/psum | solution.py:108
  436.9 1.7 copy.151
  438.6 1.9 copy.152
  (146 shorter events, 25.4 us)
Async XLA Ops:
  7.2 1.5 copy-start
  7.2 429.7 %all-reduce.5.cloned.1.call-start = ((), (), s32[]{:S(2)}) async-start(), calls=%async_computation | async-start | bytes 1769472 | tf_op jit(solution)/shard_map/psum | solution.py:108
  8.7 1.4 copy-start.10
  10.1 3.7 copy-start.1
  12.2 1.7 copy-start.30
  41.6 6.1 %collective-permute-start = (f32[1,130,128]{2,1,0:T(8,128)S(1)}, f32[1,130,128]{2,1,0:T(8,128)S(1)}, u32[]{:S(2)}, u32[]{:S(2)}) collective-permute-start(f32[1,130,128]{2,1,0:T(8,128)S(1)} %slice_select_fusion), channel_id=1, source_target_pairs={{0,32},{32,64},{64,96},{96,128},{128,160},{160,192},{192,224},{224... | collective-permute-start | bytes 199688 | tf_op jit(solution)/shard_map/ppermute | solution.py:21
  47.7 8.9 %collective-permute-start.1 = (f32[130,128]{1,0:T(8,128)S(1)}, f32[130,128]{1,0:T(8,128)S(1)}, u32[]{:S(2)}, u32[]{:S(2)}) collective-permute-start(f32[130,128]{1,0:T(8,128)S(1)} %get-tuple-element.325), channel_id=1, source_target_pairs={{0,16},{1,17},{2,18},{3,19},{4,20},{5,21},{6,22},{7,23},{8,24},{9,... | collective-permute-start | bytes 199688 | tf_op jit(solution)/shard_map/ppermute | solution.py:12
  54.8 3.5 collective-permute-start.2
  56.6 7.5 %copy-start.18 = (bf16[16,128,64]{1,2,0:T(8,128)(2,1)S(1)}, bf16[16,128,64]{1,2,0:T(8,128)(2,1)}, u32[]{:S(2)}) copy-start(bf16[16,128,64]{1,2,0:T(8,128)(2,1)} %param.57) | copy-start | bytes 786436
  58.3 6.6 %collective-permute-start.3 = (f32[20,1,128]{2,1,0:T(1,128)S(1)}, f32[20,1,128]{2,1,0:T(1,128)S(1)}, u32[]{:S(2)}, u32[]{:S(2)}) collective-permute-start(f32[20,1,128]{2,1,0:T(1,128)S(1)} %get-tuple-element.321), channel_id=1, source_target_pairs={{0,1},{1,2},{2,3},{3,4},{4,5},{5,6},{6,7},{7,8},{8,9},{9,10},{10,1... | collective-permute-start | bytes 30728 | tf_op jit(solution)/shard_map/ppermute | solution.py:21
  64.1 4.6 %collective-permute-start.4 = (f32[20,1,128]{2,1,0:T(1,128)S(1)}, f32[20,1,128]{2,1,0:T(1,128)S(1)}, u32[]{:S(2)}, u32[]{:S(2)}) collective-permute-start(f32[20,1,128]{2,1,0:T(1,128)S(1)} %get-tuple-element.322), channel_id=1, source_target_pairs={{1,0},{2,1},{3,2},{4,3},{5,4},{6,5},{7,6},{8,7},{9,8},{10,9},{11,1... | collective-permute-start | bytes 30728 | tf_op jit(solution)/shard_map/ppermute | solution.py:24
  64.4 77.8 %copy-start.7 = (bf16[16,128,64]{2,1,0:T(8,128)(2,1)}, bf16[16,128,64]{2,1,0:T(8,128)(2,1)S(1)}, u32[]{:S(2)}) copy-start(bf16[16,128,64]{2,1,0:T(8,128)(2,1)S(1)} %copy.62) | copy-start | bytes 786436
  69.0 1.0 copy-start.17
  71.0 2.5 copy-start.24
  72.7 69.5 %copy-start.2 = (bf16[16,128,128]{2,1,0:T(8,128)(2,1)}, bf16[16,128,128]{2,1,0:T(8,128)(2,1)S(1)}, u32[]{:S(2)}) copy-start(bf16[16,128,128]{2,1,0:T(8,128)(2,1)S(1)} %get-tuple-element.333) | copy-start | bytes 1572868
  81.2 55.0 %collective-permute-start.10 = (bf16[1,128,192]{2,1,0:T(8,128)(2,1)S(1)}, bf16[1,128,192]{2,1,0:T(8,128)(2,1)S(1)}, u32[]{:S(2)}, u32[]{:S(2)}) collective-permute-start(bf16[1,128,192]{2,1,0:T(8,128)(2,1)S(1)} %get-tuple-element.331), channel_id=1, source_target_pairs={{0,32},{32,64},{64,96},{96,128},{128,160},{160,192},{192,224},{224... | collective-permute-start | bytes 147464 | tf_op jit(solution)/shard_map/ppermute | solution.py:21
  81.3 54.9 %collective-permute-start.11 = (bf16[1,128,192]{2,1,0:T(8,128)(2,1)S(1)}, bf16[1,128,192]{2,1,0:T(8,128)(2,1)S(1)}, u32[]{:S(2)}, u32[]{:S(2)}) collective-permute-start(bf16[1,128,192]{2,1,0:T(8,128)(2,1)S(1)} %get-tuple-element.332), channel_id=1, source_target_pairs={{32,0},{64,32},{96,64},{128,96},{160,128},{192,160},{224,192},{0,2... | collective-permute-start | bytes 147464 | tf_op jit(solution)/shard_map/ppermute | solution.py:24
  130.1 6.0 %collective-permute-start.5 = (f32[1,130,64]{1,2,0:T(8,128)S(1)}, f32[1,130,64]{1,2,0:T(8,128)S(1)}, u32[]{:S(2)}, u32[]{:S(2)}) collective-permute-start(f32[1,130,64]{1,2,0:T(8,128)S(1)} %slice_select_fusion.1), channel_id=1, source_target_pairs={{0,32},{32,64},{64,96},{96,128},{128,160},{160,192},{192,224},{224... | collective-permute-start | bytes 99848 | tf_op jit(solution)/shard_map/ppermute | solution.py:21
  136.3 5.9 %collective-permute-start.12 = (bf16[18,1,192]{2,1,0:T(2,128)(2,1)S(1)}, bf16[18,1,192]{2,1,0:T(2,128)(2,1)S(1)}, u32[]{:S(2)}, u32[]{:S(2)}) collective-permute-start(bf16[18,1,192]{2,1,0:T(2,128)(2,1)S(1)} %get-tuple-element.328), channel_id=1, source_target_pairs={{0,1},{1,2},{2,3},{3,4},{4,5},{5,6},{6,7},{7,8},{8,9},{9,10},{10,1... | collective-permute-start | bytes 20744 | tf_op jit(solution)/shard_map/ppermute | solution.py:21
  137.4 4.8 %collective-permute-start.13 = (bf16[18,1,192]{2,1,0:T(2,128)(2,1)S(1)}, bf16[18,1,192]{2,1,0:T(2,128)(2,1)S(1)}, u32[]{:S(2)}, u32[]{:S(2)}) collective-permute-start(bf16[18,1,192]{2,1,0:T(2,128)(2,1)S(1)} %get-tuple-element.329), channel_id=1, source_target_pairs={{1,0},{2,1},{3,2},{4,3},{5,4},{6,5},{7,6},{8,7},{9,8},{10,9},{11,1... | collective-permute-start | bytes 20744 | tf_op jit(solution)/shard_map/ppermute | solution.py:24
  137.4 22.9 %collective-permute-start.6 = (f32[130,64]{0,1:T(8,128)S(1)}, f32[130,64]{0,1:T(8,128)S(1)}, u32[]{:S(2)}, u32[]{:S(2)}) collective-permute-start(f32[130,64]{0,1:T(8,128)S(1)} %get-tuple-element.330), channel_id=1, source_target_pairs={{0,16},{1,17},{2,18},{3,19},{4,20},{5,21},{6,22},{7,23},{8,24},{9,... | collective-permute-start | bytes 99848 | tf_op jit(solution)/shard_map/ppermute | solution.py:12
  142.2 18.2 %collective-permute-start.7 = (f32[1,130,64]{1,2,0:T(8,128)S(1)}, f32[1,130,64]{1,2,0:T(8,128)S(1)}, u32[]{:S(2)}, u32[]{:S(2)}) collective-permute-start(f32[1,130,64]{1,2,0:T(8,128)S(1)} %get-tuple-element.318), channel_id=1, source_target_pairs={{32,0},{64,32},{96,64},{128,96},{160,128},{192,160},{224,192},{0,2... | collective-permute-start | bytes 99848 | tf_op jit(solution)/shard_map/ppermute | solution.py:24
  142.2 15.5 %copy-start.20 = (bf16[18,1,192]{2,1,0:T(2,128)(2,1)}, bf16[18,1,192]{2,1,0:T(2,128)(2,1)S(1)}, u32[]{:S(2)}) copy-start(bf16[18,1,192]{2,1,0:T(2,128)(2,1)S(1)} %collective-permute-done.12) | copy-start | bytes 20740
  142.2 16.4 %copy-start.22 = (bf16[18,1,192]{2,1,0:T(2,128)(2,1)}, bf16[18,1,192]{2,1,0:T(2,128)(2,1)S(1)}, u32[]{:S(2)}) copy-start(bf16[18,1,192]{2,1,0:T(2,128)(2,1)S(1)} %collective-permute-done.13) | copy-start | bytes 20740
  143.1 1.0 copy-start.3
  143.1 1.2 copy-start.8
  143.1 1.9 copy-start.11
  151.0 23.8 %collective-permute-start.14 = (bf16[130,192]{1,0:T(8,128)(2,1)}, bf16[130,192]{1,0:T(8,128)(2,1)}, u32[]{:S(2)}, u32[]{:S(2)}) collective-permute-start(bf16[130,192]{1,0:T(8,128)(2,1)} %get-tuple-element.326), channel_id=1, source_target_pairs={{0,16},{1,17},{2,18},{3,19},{4,20},{5,21},{6,22},{7,23},{8,24},{9,... | collective-permute-start | bytes 149768 | tf_op jit(solution)/shard_map/ppermute | solution.py:12
  160.5 1.3 copy-start.5
  162.0 9.2 %copy-start.6 = (f32[20,130,64]{1,2,0:T(8,128)S(1)}, f32[20,130,64]{1,2,0:T(8,128)}, u32[]{:S(2)}) copy-start(f32[20,130,64]{1,2,0:T(8,128)} %copy-done.5) | copy-start | bytes 1996804
  162.0 3.8 collective-permute-start.8
  164.1 5.2 %collective-permute-start.9 = (f32[20,1,64]{2,1,0:T(1,128)}, f32[20,1,64]{2,1,0:T(1,128)}, u32[]{:S(2)}, u32[]{:S(2)}) collective-permute-start(f32[20,1,64]{2,1,0:T(1,128)} %copy.59), channel_id=1, source_target_pairs={{1,0},{2,1},{3,2},{4,3},{5,4},{6,5},{7,6},{8,7},{9,8},{10,9},{11,1... | collective-permute-start | bytes 15368 | tf_op jit(solution)/shard_map/ppermute | solution.py:24
  173.0 1.1 copy-start.13
  173.0 1.3 copy-start.14
  174.4 1.0 copy-start.4
  174.4 1.6 copy-start.9
  174.5 1.6 copy-start.21
  174.5 1.6 copy-start.23
  174.6 3.0 copy-start.15
  174.6 2.4 copy-start.12
  179.5 0.8 copy-start.28
  179.5 0.9 copy-start.29
  179.6 1.0 copy-start.19
  180.4 1.0 copy-start.25
  180.4 1.0 copy-start.26
  180.4 1.0 copy-start.27
  180.5 1.7 copy-start.16
Sparse Core Ops, SparseCore 0:
  182.3 254.5 all-reduce.4
where the time goes:
time: 449 us; the launch traced here: 447 us
  waiting for transfers between devices  267 us (59%)
  local copies, waits for them, and re-layouts  69.3 us (15%)
  other arithmetic  44.8 us (10%)
  starting transfers between devices  32.6 us (7%)
  matrix products  18.6 us (4%)
  between operations  14.9 us (3%)
    psum x1, waiting for transfers between devices, body(): lax.psum((local_first, local_second), ('lat', 'lon'))  251 us
    scatter-add x14, local copies, waits for them, and re-layouts, spread(): grid = grid.at[a:a + rows, b:b + cols].add(terms[:, :, a, b])  46.2 us
    add x10, other arithmetic, spread(): grid = grid.at[a:a + rows, b:b + cols].add(terms[:, :, a, b])  18.6 us
    ppermute x3, starting transfers between devices, passed_along(): lax.ppermute(shard, axis, [(i, (i + by) % peers) for i in range(peers)])  17.3 us
    dot_general x18, matrix products, taps_product(): lax.dot_general(piece, flat, (((0,), (0,)), ((), ())), preferred_element_...  14.2 us
    ppermute x6, starting transfers between devices, extended(): lax.ppermute(lax.slice_in_dim(block, block.shape[dim] - width, None, axis...  9.36 us
    unnamed x69, local copies, waits for them, and re-layouts  9.2 us
  transfers between devices with their start and end apart: 16, of which 8 were waited for; matrix products, arithmetic and copies ran while one was open for 16% of the time, Pallas kernels for 0%

commit v1 on v0

--- a/solution.py
+++ b/solution.py
@@ -105,7 +105,7 @@
     grad_pre = (grad_act * slope).astype(jnp.bfloat16)
     local_first = taps_product(padded_in, grad_pre)
     grad_inputs = fold_grads(spread(grad_pre, w_first)).astype(jnp.bfloat16)
-    grad_w_first, grad_w_second = lax.psum((local_first, local_second), ("lat", "lon"))
+    grad_w_first, grad_w_second = lax.psum(lax.psum((local_first, local_second), "lat"), "lon")
     return (grad_inputs, grad_w_first, grad_w_second)
 
 

time: 449 us -> 516 us (1.15)
  waiting for transfers between devices: 267 us -> 347 us
  matrix products: 18.6 us -> 10.4 us
    psum x1 -> x2, waiting for transfers between devices: 251 us -> 329 us  [the longest x1 264 us: body(): lax.psum(lax.psum((local_first, local_second), 'lat'), 'lon')]
    ppermute x6, starting transfers between devices: 9.36 us -> 15.9 us  [extended(): lax.ppermute(lax.slice_in_dim(block, block.shape[dim] - width, None, axis...]
    dot_general x18, matrix products: 14.2 us -> 8.21 us  [taps_product(): lax.dot_general(piece, flat, (((0,), (0,)), ((), ())), preferred_element_...]
  transfers between devices with their start and end apart: 16 -> 17, of which waited for: 8 -> 10; matrix products, arithmetic and copies ran while one was open for 16% -> 13% of each run, Pallas kernels for 0% -> 0%
where the time goes in v1:
time: 516 us; the launch traced here: 515 us
  waiting for transfers between devices  347 us (67%)
  local copies, waits for them, and re-layouts  64.6 us (13%)
  other arithmetic  41.2 us (8%)
  starting transfers between devices  36.6 us (7%)
  between operations  14.8 us (3%)
  matrix products  10.4 us (2%)
    psum x1, waiting for transfers between devices, body(): lax.psum(lax.psum((local_first, local_second), 'lat'), 'lon')  264 us
    psum x1, waiting for transfers between devices, body(): lax.psum((local_first, local_second), 'lat')  64.7 us
    scatter-add x14, local copies, waits for them, and re-layouts, spread(): grid = grid.at[a:a + rows, b:b + cols].add(terms[:, :, a, b])  45.7 us
    add x10, other arithmetic, spread(): grid = grid.at[a:a + rows, b:b + cols].add(terms[:, :, a, b])  17.5 us
    ppermute x6, starting transfers between devices, extended(): lax.ppermute(lax.slice_in_dim(block, block.shape[dim] - width, None, axis...  15.9 us
    ppermute x3, starting transfers between devices, passed_along(): lax.ppermute(shard, axis, [(i, (i + by) % peers) for i in range(peers)])  13.6 us
  transfers between devices with their start and end apart: 17, of which 10 were waited for; matrix products, arithmetic and copies ran while one was open for 13% of the time, Pallas kernels for 0%

profile of v1, /device:TPU:1, one launch (start us, length us, event | category | flops | bytes accessed | tf_op | source)
XLA Modules:
  0.0 514.8 jit_solution(5425706115646145299)
XLA Ops:
  7.2 1.0 broadcast_multiply_fusion
  8.7 1.4 fusion.71
  10.9 1.0 fusion.104
  12.0 1.6 fusion.17
  14.4 3.4 scatter-add.89
  17.8 3.1 add_select_fusion
  20.9 3.3 scatter-add.90
  24.2 1.4 fusion.16
  25.7 1.3 fusion.14
  27.0 2.1 scatter-add.94
  29.1 1.3 fusion.13
  30.5 2.1 scatter-add.95
  32.6 1.4 fusion.12
  34.1 1.4 fusion.10
  35.4 2.1 scatter-add.99
  37.6 1.4 fusion.9
  38.9 2.1 scatter-add.100
  41.1 2.2 collective-permute-start
  43.3 3.9 collective-permute-done
  47.2 7.1 %collective-permute-start.1 = (f32[130,128]{1,0:T(8,128)S(1)}, f32[130,128]{1,0:T(8,128)S(1)}, u32[]{:S(2)}, u32[]{:S(2)}) collective-permute-start(f32[130,128]{1,0:T(8,128)S(1)} %get-tuple-element.327), channel_id=1, source_target_pairs={{0,16},{1,17},{2,18},{3,19},{4,20},{5,21},{6,22},{7,23},{8,24},{9,... | collective-permute-start | bytes 199688 | tf_op jit(solution)/shard_map/ppermute | solution.py:12
  54.2 1.4 collective-permute-start.2
  56.2 1.5 collective-permute-done.2
  57.7 5.8 %collective-permute-start.3 = (f32[20,1,128]{2,1,0:T(1,128)S(1)}, f32[20,1,128]{2,1,0:T(1,128)S(1)}, u32[]{:S(2)}, u32[]{:S(2)}) collective-permute-start(f32[20,1,128]{2,1,0:T(1,128)S(1)} %get-tuple-element.323), channel_id=1, source_target_pairs={{0,1},{1,2},{2,3},{3,4},{4,5},{5,6},{6,7},{7,8},{8,9},{9,10},{10,1... | collective-permute-start | bytes 30728 | tf_op jit(solution)/shard_map/ppermute | solution.py:21
  63.6 1.2 copy.62
  64.8 3.4 collective-permute-done.4
  68.4 1.1 slice.1054
  69.5 1.5 scatter-add.105
  71.0 0.9 slice_add_fusion.2
  71.9 1.5 scatter-add.106
  73.4 2.0 fusion.8
  75.4 0.8 fusion.69
  76.2 2.3 fusion.68
  79.9 6.0 %scatter-add.110 = f32[18,130,64]{1,2,0:T(8,128)S(1)} dynamic-update-slice(f32[18,130,64]{1,2,0:T(8,128)S(1)} %scatter-add.109, f32[16,128,64]{1,2,0:T(8,128)} %fusion.68, s32[]{:T(128)} %bitcast.10, s32[]{:T(128)} %bitcast.11, s32[]{:T(128)} %constant.655.clone.1) | dynamic-update-slice | bytes 1048580 | tf_op jit(solution)/shard_map/scatter-add | solution.py:89
  85.9 3.8 add_select_fusion.1
  89.7 5.9 %scatter-add.111 = f32[18,130,64]{1,2,0:T(8,128)S(1)} dynamic-update-slice(f32[18,130,64]{1,2,0:T(8,128)S(1)} %scatter-add.110, f32[16,128,64]{1,2,0:T(8,128)} %add_select_fusion.1, s32[]{:T(128)} %bitcast.13, s32[]{:T(128)} %bitcast.14, s32[]{:T(128)} %constant.655.clone.1) | dynamic-update-slice | bytes 1048580 | tf_op jit(solution)/shard_map/scatter-add | solution.py:89
  95.5 1.2 fusion.67
  96.7 2.0 fusion.65
  98.8 4.7 scatter-add.115
  103.4 2.0 fusion.64
  105.5 4.7 scatter-add.116
  110.2 1.2 fusion.63
  111.3 2.0 fusion.61
  113.4 4.7 scatter-add.120
  118.1 2.1 fusion.60
  120.1 4.7 scatter-add.121
  124.8 1.1 collective-permute-start.5
  126.1 2.7 collective-permute-start.11
  128.8 2.3 collective-permute-done.5
  131.8 1.2 collective-permute-start.12
  133.7 4.4 collective-permute-start.6
  138.0 2.2 collective-permute-start.7
  140.2 0.8 pad_maximum_fusion.2
  141.3 0.9 copy-done.6
  145.0 2.2 collective-permute-start.14
  149.9 3.0 collective-permute-done.14
  155.9 0.9 pad_maximum_fusion.3
  158.3 5.6 %collective-permute-start.8 = (f32[20,1,64]{2,1,0:T(1,128)S(1)}, f32[20,1,64]{2,1,0:T(1,128)S(1)}, u32[]{:S(2)}, u32[]{:S(2)}) collective-permute-start(f32[20,1,64]{2,1,0:T(1,128)S(1)} %copy.58), channel_id=1, source_target_pairs={{0,1},{1,2},{2,3},{3,4},{4,5},{5,6},{6,7},{7,8},{8,9},{9,10},{10,1... | collective-permute-start | bytes 15368 | tf_op jit(solution)/shard_map/ppermute | solution.py:21
  164.1 0.8 collective-permute-start.9
  165.3 3.8 collective-permute-done.9
  169.3 64.7 %all-reduce.9.cloned.1.call-done = (f32[3,3,64,128]{3,2,1,0:T(8,128)}, f32[3,3,128,128]{3,2,1,0:T(8,128)}) async-done(((f32[3,3,64,128]{3,2,1,0:T(8,128)}, f32[3,3,128,128]{3,2,1,0:T(8,128)}), (f32[3,3,64,128]{3,2,1,0:T(8,128)}, f32[3,3,128,128]{3,2,1,0:T(8,128)})) %all-reduce.9.cloned.1.call-update) | async-done | bytes 884752 | tf_op jit(solution)/shard_map/psum | solution.py:108
  237.6 1.9 scatter-add.129
  240.3 264.1 %all-reduce.7.cloned.1.call-done = (f32[3,3,64,128]{3,2,1,0:T(8,128)}, f32[3,3,128,128]{3,2,1,0:T(8,128)}) async-done(((f32[3,3,64,128]{3,2,1,0:T(8,128)}, f32[3,3,128,128]{3,2,1,0:T(8,128)}), (f32[3,3,64,128]{3,2,1,0:T(8,128)}, f32[3,3,128,128]{3,2,1,0:T(8,128)})) %all-reduce.7.cloned.1.call-update) | async-done | bytes 884752 | tf_op jit(solution)/shard_map/psum | solution.py:108
  504.4 1.7 copy.153
  506.1 1.9 copy.154
  (111 shorter events, 21.3 us)
Async XLA Ops:
  7.2 1.5 copy-start
  7.2 226.8 %all-reduce.9.cloned.1.call-start = ((), (), s32[]{:S(2)}) async-start(), calls=%async_computation.1 | async-start | bytes 1769472 | tf_op jit(solution)/shard_map/psum | solution.py:108
  8.7 1.4 copy-start.4
  10.1 3.6 copy-start.1
  12.0 1.7 copy-start.11
  41.1 6.1 %collective-permute-start = (f32[1,130,128]{2,1,0:T(8,128)S(1)}, f32[1,130,128]{2,1,0:T(8,128)S(1)}, u32[]{:S(2)}, u32[]{:S(2)}) collective-permute-start(f32[1,130,128]{2,1,0:T(8,128)S(1)} %slice_select_fusion), channel_id=1, source_target_pairs={{0,32},{32,64},{64,96},{96,128},{128,160},{160,192},{192,224},{224... | collective-permute-start | bytes 199688 | tf_op jit(solution)/shard_map/ppermute | solution.py:21
  47.2 8.9 %collective-permute-start.1 = (f32[130,128]{1,0:T(8,128)S(1)}, f32[130,128]{1,0:T(8,128)S(1)}, u32[]{:S(2)}, u32[]{:S(2)}) collective-permute-start(f32[130,128]{1,0:T(8,128)S(1)} %get-tuple-element.327), channel_id=1, source_target_pairs={{0,16},{1,17},{2,18},{3,19},{4,20},{5,21},{6,22},{7,23},{8,24},{9,... | collective-permute-start | bytes 199688 | tf_op jit(solution)/shard_map/ppermute | solution.py:12
  54.2 3.5 collective-permute-start.2
  57.7 7.1 %collective-permute-start.3 = (f32[20,1,128]{2,1,0:T(1,128)S(1)}, f32[20,1,128]{2,1,0:T(1,128)S(1)}, u32[]{:S(2)}, u32[]{:S(2)}) collective-permute-start(f32[20,1,128]{2,1,0:T(1,128)S(1)} %get-tuple-element.323), channel_id=1, source_target_pairs={{0,1},{1,2},{2,3},{3,4},{4,5},{5,6},{6,7},{7,8},{8,9},{9,10},{10,1... | collective-permute-start | bytes 30728 | tf_op jit(solution)/shard_map/ppermute | solution.py:21
  63.6 4.6 collective-permute-start.4
  73.4 2.0 copy-start.10
  76.2 3.2 copy-start.3
  78.6 1.0 copy-start.5
  79.4 52.3 %collective-permute-start.10 = (bf16[1,128,192]{2,1,0:T(8,128)(2,1)}, bf16[1,128,192]{2,1,0:T(8,128)(2,1)S(1)}, u32[]{:S(2)}, u32[]{:S(2)}) collective-permute-start(bf16[1,128,192]{2,1,0:T(8,128)(2,1)} %get-tuple-element.333), channel_id=1, source_target_pairs={{0,32},{32,64},{64,96},{96,128},{128,160},{160,192},{192,224},{224... | collective-permute-start | bytes 147464 | tf_op jit(solution)/shard_map/ppermute | solution.py:21
  118.0 7.9 %copy-start.9 = (bf16[16,128,64]{1,2,0:T(8,128)(2,1)S(1)}, bf16[16,128,64]{1,2,0:T(8,128)(2,1)}, u32[]{:S(2)}) copy-start(bf16[16,128,64]{1,2,0:T(8,128)(2,1)} %param.57) | copy-start | bytes 786436
  124.8 6.3 %collective-permute-start.5 = (f32[1,130,64]{1,2,0:T(8,128)S(1)}, f32[1,130,64]{1,2,0:T(8,128)S(1)}, u32[]{:S(2)}, u32[]{:S(2)}) collective-permute-start(f32[1,130,64]{1,2,0:T(8,128)S(1)} %slice_select_fusion.1), channel_id=1, source_target_pairs={{0,32},{32,64},{64,96},{96,128},{128,160},{160,192},{192,224},{224... | collective-permute-start | bytes 99848 | tf_op jit(solution)/shard_map/ppermute | solution.py:21
  126.1 5.6 %collective-permute-start.11 = (bf16[1,128,192]{2,1,0:T(8,128)(2,1)S(1)}, bf16[1,128,192]{2,1,0:T(8,128)(2,1)S(1)}, u32[]{:S(2)}, u32[]{:S(2)}) collective-permute-start(bf16[1,128,192]{2,1,0:T(8,128)(2,1)S(1)} %get-tuple-element.334), channel_id=1, source_target_pairs={{32,0},{64,32},{96,64},{128,96},{160,128},{192,160},{224,192},{0,2... | collective-permute-start | bytes 147464 | tf_op jit(solution)/shard_map/ppermute | solution.py:24
  131.8 8.4 %collective-permute-start.12 = (bf16[18,1,192]{2,1,0:T(2,128)(2,1)S(1)}, bf16[18,1,192]{2,1,0:T(2,128)(2,1)S(1)}, u32[]{:S(2)}, u32[]{:S(2)}) collective-permute-start(bf16[18,1,192]{2,1,0:T(2,128)(2,1)S(1)} %get-tuple-element.330), channel_id=1, source_target_pairs={{0,1},{1,2},{2,3},{3,4},{4,5},{5,6},{6,7},{7,8},{8,9},{9,10},{10,1... | collective-permute-start | bytes 20744 | tf_op jit(solution)/shard_map/ppermute | solution.py:21
  133.0 7.2 %collective-permute-start.13 = (bf16[18,1,192]{2,1,0:T(2,128)(2,1)S(1)}, bf16[18,1,192]{2,1,0:T(2,128)(2,1)S(1)}, u32[]{:S(2)}, u32[]{:S(2)}) collective-permute-start(bf16[18,1,192]{2,1,0:T(2,128)(2,1)S(1)} %get-tuple-element.331), channel_id=1, source_target_pairs={{1,0},{2,1},{3,2},{4,3},{5,4},{6,5},{7,6},{8,7},{9,8},{10,9},{11,1... | collective-permute-start | bytes 20744 | tf_op jit(solution)/shard_map/ppermute | solution.py:24
  133.7 15.6 %collective-permute-start.6 = (f32[130,64]{0,1:T(8,128)S(1)}, f32[130,64]{0,1:T(8,128)S(1)}, u32[]{:S(2)}, u32[]{:S(2)}) collective-permute-start(f32[130,64]{0,1:T(8,128)S(1)} %get-tuple-element.332), channel_id=1, source_target_pairs={{0,16},{1,17},{2,18},{3,19},{4,20},{5,21},{6,22},{7,23},{8,24},{9,... | collective-permute-start | bytes 99848 | tf_op jit(solution)/shard_map/ppermute | solution.py:12
  138.0 19.7 %collective-permute-start.7 = (f32[1,130,64]{1,2,0:T(8,128)}, f32[1,130,64]{1,2,0:T(8,128)S(1)}, u32[]{:S(2)}, u32[]{:S(2)}) collective-permute-start(f32[1,130,64]{1,2,0:T(8,128)} %get-tuple-element.320), channel_id=1, source_target_pairs={{32,0},{64,32},{96,64},{128,96},{160,128},{192,160},{224,192},{0,2... | collective-permute-start | bytes 99848 | tf_op jit(solution)/shard_map/ppermute | solution.py:24
  141.1 1.0 copy-start.6
  145.0 7.9 %collective-permute-start.14 = (bf16[130,192]{1,0:T(8,128)(2,1)S(1)}, bf16[130,192]{1,0:T(8,128)(2,1)S(1)}, u32[]{:S(2)}, u32[]{:S(2)}) collective-permute-start(bf16[130,192]{1,0:T(8,128)(2,1)S(1)} %get-tuple-element.328), channel_id=1, source_target_pairs={{0,16},{1,17},{2,18},{3,19},{4,20},{5,21},{6,22},{7,23},{8,24},{9,... | collective-permute-start | bytes 149768 | tf_op jit(solution)/shard_map/ppermute | solution.py:12
  155.9 1.7 copy-start.2
  157.6 346.8 %all-reduce.7.cloned.1.call-start = ((), (), s32[]{:S(2)}) async-start(), calls=%async_computation | async-start | bytes 1769472 | tf_op jit(solution)/shard_map/psum | solution.py:108
  158.3 6.7 %collective-permute-start.8 = (f32[20,1,64]{2,1,0:T(1,128)S(1)}, f32[20,1,64]{2,1,0:T(1,128)S(1)}, u32[]{:S(2)}, u32[]{:S(2)}) collective-permute-start(f32[20,1,64]{2,1,0:T(1,128)S(1)} %copy.58), channel_id=1, source_target_pairs={{0,1},{1,2},{2,3},{3,4},{4,5},{5,6},{6,7},{7,8},{8,9},{9,10},{10,1... | collective-permute-start | bytes 15368 | tf_op jit(solution)/shard_map/ppermute | solution.py:21
  164.1 4.9 collective-permute-start.9
  234.9 1.0 copy-start.7
  236.1 1.2 copy-start.8
Sparse Core Ops, SparseCore 0:
  157.7 76.2 all-reduce.8
  236.9 267.4 all-reduce.6
